TPU v7x, 32 devices: a whole 2x2x4 slice. The times are simulated.
32 devices in a mesh: batch: 16 (over z, x, core), seg: 2 (over y).
Axes of the slice: x: 2, y: 2, z: 4, core: 2. Of those that a mesh axis runs over, the one named last changes fastest.
Arguments:
- tokens: bfloat16 [32, 2, 512, 768], P('batch', 'seg'), may hold values from -6 to 6
- start_memory: float32 [32, 256, 768], P('batch', None, 'seg'), may hold values from -6 to 6
- has_memory: int32 [32], P('batch'), may hold values 0 or 1
- sticky: int32 [32, 2, 512], P('batch', 'seg'), may hold values from 0 to 4095
- w_qkv: bfloat16 [768, 2304], replicated, may hold values from -0.21875 to 0.21875
- w_out: bfloat16 [768, 768], replicated, may hold values from -3 to 3
- w_in: bfloat16 [768, 3072], replicated, may hold values from -0.21875 to 0.21875
- w_back: bfloat16 [3072, 768], replicated, may hold values from -0.109375 to 0.109375
- q_bias: float32 [768], replicated, may hold values from -3 to 3
- v_bias: float32 [768], replicated, may hold values from -3 to 3
- out_bias: float32 [768], replicated, may hold values from -3 to 3
- in_bias: float32 [3072], replicated, may hold values from -3 to 3
- back_bias: float32 [768], replicated, may hold values from -3 to 3
- ln1_gain: float32 [768], replicated, may hold values from 0.5 to 1.5
- ln1_bias: float32 [768], replicated, may hold values from -2 to 2
- ln2_gain: float32 [768], replicated, may hold values from 0.5 to 1.5
- ln2_bias: float32 [768], replicated, may hold values from -2 to 2
- cotangent: bfloat16 [32, 2, 512, 768], P('batch', 'seg'), may hold values from -6 to 6
Outputs:
- result: bfloat16 [32, 2, 512, 768], P('batch', 'seg')
- input_grad: bfloat16 [32, 2, 512, 768], P('batch', 'seg')
- start_memory_grad: float32 [32, 256, 768], P('batch', None, 'seg')
- grad_qkv: float32 [768, 2304], P('batch')
- grad_out: float32 [768, 768], P('batch')
- grad_in: float32 [768, 3072], P('batch')
- grad_back: float32 [3072, 768], P('batch')
- grad_q_bias: float32 [768], P('batch')
- grad_v_bias: float32 [768], P('batch')
- grad_out_bias: float32 [768], P('batch')
- grad_in_bias: float32 [3072], P('batch')
- grad_back_bias: float32 [768], P('batch')
- grad_ln1_gain: float32 [768], P('batch')
- grad_ln1_bias: float32 [768], P('batch')
- grad_ln2_gain: float32 [768], P('batch')
- grad_ln2_bias: float32 [768], P('batch')
Inputs may be any that keep to these rules, and one draw needn't show every extreme that they name: `sticky`: grid indices of the 512 points at which each segment samples the previous memory signal. `has_memory`: 1 where a document begins with its given memory coefficients, 0 where its memory begins empty.
All inputs are finite; a program needn't handle non-finite values. No bound on the sum of `has_memory` on one device may be relied on, other than what follows from the above.
Results may differ from a plain program's by a relative error of at most 0.012.
Values sent between devices are 32-bit elements; how exact they have to be, the bound alone decides.
A program may use at most 256 MiB of HBM per device.

v0:
```python
import math

import jax
import jax.numpy as jnp
from jax import lax
from jax.sharding import PartitionSpec as P

HEADS = 12
HD = 64
NB = 256
L = 512
STICKY = 512
GRID = 4096


EPSILON = 1e-05
RIDGE = 0.5
MASKED = -1e30
PRECISE = lax.Precision.HIGHEST


def shifted_2(block, axis, distance):
    devices = range(lax.axis_size(axis))
    route = [(i - distance, i) for i in devices if i - distance in devices]
    return lax.ppermute(block, axis, route)


def precise(left, right):
    return jnp.dot(left, right, precision=PRECISE)


def layer_norm(values, gain, offset):
    center = jnp.mean(values, -1, keepdims=True)
    shifted = values - center
    spread = jnp.mean(shifted * shifted, -1, keepdims=True)
    return shifted * lax.rsqrt(spread + EPSILON) * gain + offset


def gelu_tanh(values):
    return jax.nn.gelu(values, approximate=True)


def basis_at(points):
    centers = (jnp.arange(NB, dtype=jnp.float32) + 0.5) / NB
    scaled = (points[None, :] - centers[:, None]) * NB
    return jnp.exp(-0.5 * scaled * scaled)


def memory_maps(positions):
    old_times = (positions.astype(jnp.float32) + 0.5) / GRID
    new_times = 0.5 + 0.5 * (jnp.arange(L, dtype=jnp.float32) + 0.5) / L
    design = jnp.concatenate([basis_at(0.5 * old_times), basis_at(new_times)], axis=1)
    gram = precise(design, design.T) + RIDGE * jnp.eye(NB, dtype=jnp.float32)
    factor = jnp.linalg.cholesky(gram)
    solved = jax.scipy.linalg.cho_solve((factor, True), design)
    carry_map = precise(solved[:, :STICKY], basis_at(old_times).T)
    return (carry_map, solved[:, STICKY:])


def visible():
    row_ids = jnp.arange(L)[:, None]
    col_ids = jnp.arange(L + NB)[None, :]
    return (col_ids >= L) | (col_ids <= row_ids)


def shards(
    tokens,
    start_memory,
    has_memory,
    sticky,
    w_qkv,
    w_out,
    w_in,
    w_back,
    q_bias,
    v_bias,
    out_bias,
    in_bias,
    back_bias,
    ln1_gain,
    ln1_bias,
    ln2_gain,
    ln2_bias,
    cotangent,
):
    width = w_qkv.shape[0]
    full_start = lax.all_gather(start_memory, "seg", axis=2, tiled=True)
    start_flags = has_memory.astype(jnp.float32)
    is_first = lax.axis_index("seg") == 0
    chain_size = lax.axis_size("seg")
    scale_factor = HD ** (-0.5)
    allowed = visible()
    all_params = (
        w_qkv,
        w_out,
        w_in,
        w_back,
        q_bias,
        v_bias,
        out_bias,
        in_bias,
        back_bias,
        ln1_gain,
        ln1_bias,
        ln2_gain,
        ln2_bias,
    )
    empty_grads = tuple((jnp.zeros(p.shape, jnp.float32) for p in all_params))

    def attention_scores(query_heads, key_heads):
        scores = (
            jnp.einsum("lhd,khd->hlk", query_heads, key_heads, preferred_element_type=jnp.float32)
            * scale_factor
        )
        return jnp.where(allowed[None], scores, MASKED)

    def micro(totals, inputs):
        seg_tokens, positions, seg_cot, begin, flag = inputs
        carry_map, data_map = memory_maps(positions)
        token_values = seg_tokens.astype(jnp.float32)
        hidden_low = layer_norm(token_values, ln1_gain, ln1_bias).astype(jnp.bfloat16)
        fresh = precise(data_map, hidden_low.astype(jnp.float32))
        initial = flag * begin
        own_start = jnp.where(is_first, initial, jnp.zeros_like(initial))

        def down_step(step_index, incoming):
            produced = precise(carry_map, incoming) + fresh
            passed = shifted_2(produced, "seg", 1)
            return passed + own_start

        memory = lax.fori_loop(0, chain_size - 1, down_step, own_start)
        projected = jnp.dot(hidden_low, w_qkv, preferred_element_type=jnp.float32)
        mem_in = memory.astype(jnp.bfloat16)
        mem_proj = jnp.dot(mem_in, w_qkv[:, width:], preferred_element_type=jnp.float32)
        query = (projected[:, :width] + q_bias).astype(jnp.bfloat16)
        keys = jnp.concatenate([projected[:, width : 2 * width], mem_proj[:, :width]], 0).astype(
            jnp.bfloat16
        )
        values = (
            jnp.concatenate([projected[:, 2 * width :], mem_proj[:, width:]], 0) + v_bias
        ).astype(jnp.bfloat16)
        query_heads = query.reshape(L, HEADS, HD)
        key_heads = keys.reshape(L + NB, HEADS, HD)
        value_heads = values.reshape(L + NB, HEADS, HD)
        scores = attention_scores(query_heads, key_heads)
        row_peak = jnp.max(scores, -1, keepdims=True)
        weight = jnp.exp(scores - row_peak)
        row_total = jnp.sum(weight, -1, keepdims=True)
        probabilities = (weight / row_total).astype(jnp.bfloat16)
        log_total = row_peak + jnp.log(row_total)
        attended = jnp.einsum(
            "hlk,khd->lhd", probabilities, value_heads, preferred_element_type=jnp.float32
        ).reshape(L, width)
        mixed = attended.astype(jnp.bfloat16)
        residual = token_values + (
            jnp.dot(mixed, w_out, preferred_element_type=jnp.float32) + out_bias
        )
        normed_low = layer_norm(residual, ln2_gain, ln2_bias).astype(jnp.bfloat16)
        pre_act = jnp.dot(normed_low, w_in, preferred_element_type=jnp.float32) + in_bias
        activated, gelu_back = jax.vjp(gelu_tanh, pre_act)
        act_low = activated.astype(jnp.bfloat16)
        output = (
            residual + (jnp.dot(act_low, w_back, preferred_element_type=jnp.float32) + back_bias)
        ).astype(jnp.bfloat16)
        out_grad = seg_cot.astype(jnp.float32)
        back_term = jnp.einsum("lf,ld->fd", act_low, seg_cot, preferred_element_type=jnp.float32)
        back_bias_term = jnp.sum(out_grad, 0)
        act_grad = jnp.dot(seg_cot, w_back.T, preferred_element_type=jnp.float32)
        (pre_grad,) = gelu_back(act_grad)
        pre_low = pre_grad.astype(jnp.bfloat16)
        in_term = jnp.einsum("ld,lf->df", normed_low, pre_low, preferred_element_type=jnp.float32)
        in_bias_term = jnp.sum(pre_low.astype(jnp.float32), 0)
        normed_grad = jnp.dot(pre_low, w_in.T, preferred_element_type=jnp.float32)
        _, norm_two_back = jax.vjp(layer_norm, residual, ln2_gain, ln2_bias)
        residual_part, gain_two_term, bias_two_term = norm_two_back(normed_grad)
        residual_grad = out_grad + residual_part
        branch_low = residual_grad.astype(jnp.bfloat16)
        out_term = jnp.einsum("ld,le->de", mixed, branch_low, preferred_element_type=jnp.float32)
        out_bias_term = jnp.sum(branch_low.astype(jnp.float32), 0)
        mixed_grad = jnp.dot(branch_low, w_out.T, preferred_element_type=jnp.float32).astype(
            jnp.bfloat16
        )
        mixed_heads = mixed_grad.reshape(L, HEADS, HD)
        chances = jnp.exp(attention_scores(query_heads, key_heads) - log_total)
        prob_grad = jnp.einsum(
            "lhd,khd->hlk", mixed_heads, value_heads, preferred_element_type=jnp.float32
        )
        row_delta = jnp.sum(chances * prob_grad, -1, keepdims=True)
        score_low = (chances * (prob_grad - row_delta)).astype(jnp.bfloat16)
        query_grad = (
            (
                jnp.einsum("hlk,khd->lhd", score_low, key_heads, preferred_element_type=jnp.float32)
                * scale_factor
            )
            .reshape(L, width)
            .astype(jnp.bfloat16)
        )
        key_grad = (
            (
                jnp.einsum(
                    "hlk,lhd->khd", score_low, query_heads, preferred_element_type=jnp.float32
                )
                * scale_factor
            )
            .reshape(L + NB, width)
            .astype(jnp.bfloat16)
        )
        value_grad = (
            jnp.einsum(
                "hlk,lhd->khd", probabilities, mixed_heads, preferred_element_type=jnp.float32
            )
            .reshape(L + NB, width)
            .astype(jnp.bfloat16)
        )
        token_proj_grad = jnp.concatenate([query_grad, key_grad[:L], value_grad[:L]], 1)
        memory_proj_grad = jnp.concatenate([key_grad[L:], value_grad[L:]], 1)
        qkv_term = jnp.einsum(
            "ld,le->de", hidden_low, token_proj_grad, preferred_element_type=jnp.float32
        )
        qkv_term = qkv_term.at[:, width:].add(
            jnp.einsum("nd,ne->de", mem_in, memory_proj_grad, preferred_element_type=jnp.float32)
        )
        q_bias_term = jnp.sum(query_grad.astype(jnp.float32), 0)
        v_bias_term = jnp.sum(value_grad.astype(jnp.float32), 0)
        hidden_grad = jnp.dot(token_proj_grad, w_qkv.T, preferred_element_type=jnp.float32)
        local_grad = jnp.dot(
            memory_proj_grad, w_qkv[:, width:].T, preferred_element_type=jnp.float32
        )
        carry_back = carry_map.T

        def up_step(step_index, incoming):
            produced_grad = precise(carry_back, incoming) + local_grad
            return shifted_2(produced_grad, "seg", -1)

        incoming_grad = lax.fori_loop(0, chain_size - 1, up_step, jnp.zeros_like(local_grad))
        hidden_grad = hidden_grad + precise(data_map.T, incoming_grad)
        _, norm_one_back = jax.vjp(layer_norm, token_values, ln1_gain, ln1_bias)
        token_part, gain_one_term, bias_one_term = norm_one_back(hidden_grad)
        input_grad = (residual_grad + token_part).astype(jnp.bfloat16)
        start_grad = jnp.where(
            is_first, flag * (local_grad + precise(carry_back, incoming_grad)), 0.0
        )
        terms = (
            qkv_term,
            out_term,
            in_term,
            back_term,
            q_bias_term,
            v_bias_term,
            out_bias_term,
            in_bias_term,
            back_bias_term,
            gain_one_term,
            bias_one_term,
            gain_two_term,
            bias_two_term,
        )
        totals = tuple((a + b for a, b in zip(totals, terms)))
        return (totals, (output, input_grad, start_grad))

    totals, (outputs, input_grads, start_grads) = lax.scan(
        micro, empty_grads, (tokens[:, 0], sticky[:, 0], cotangent[:, 0], full_start, start_flags)
    )
    start_share = lax.psum_scatter(start_grads, "seg", scatter_dimension=2, tiled=True)
    batch_count = lax.axis_size("batch")
    stacked = jnp.concatenate([g.reshape(batch_count, -1) for g in totals], 1)
    summed = lax.psum_scatter(stacked, "batch", scatter_dimension=0, tiled=True)
    summed = lax.psum(summed, "seg")
    summed = summed.reshape(-1)
    pieces = []
    offset = 0
    for param in all_params:
        length = math.prod(param.shape) // batch_count
        own_shape = (param.shape[0] // batch_count,) + tuple(param.shape[1:])
        pieces.append(summed[offset : offset + length].reshape(own_shape))
        offset = offset + length
    return (outputs[:, None], input_grads[:, None], start_share) + tuple(pieces)


def solution(mesh):
    in_specs = (
        P("batch", "seg", None, None),
        P("batch", None, "seg"),
        P("batch"),
        P("batch", "seg", None),
        P(),
        P(),
        P(),
        P(),
        P(),
        P(),
        P(),
        P(),
        P(),
        P(),
        P(),
        P(),
        P(),
        P("batch", "seg", None, None),
    )
    out_specs = (
        P("batch", "seg", None, None),
        P("batch", "seg", None, None),
        P("batch", None, "seg"),
        P("batch", None),
        P("batch", None),
        P("batch", None),
        P("batch", None),
        P("batch"),
        P("batch"),
        P("batch"),
        P("batch"),
        P("batch"),
        P("batch"),
        P("batch"),
        P("batch"),
        P("batch"),
    )
    return jax.shard_map(shards, mesh=mesh, in_specs=in_specs, out_specs=out_specs, check_vma=False)
```

profile of v0, /device:TPU:0, one launch (start us, length us, event | category | flops | bytes accessed | tf_op | source)
XLA Modules:
  0.0 1247.5 jit_solution(8575092659957771951)
XLA Ops:
  10.1 29.4 %all-gather.2.cloned.1.call-done = f32[2,256,768]{2,1,0:T(8,128)} async-done(((f32[2,256,384]{2,1,0:T(8,128)}), f32[2,256,768]{2,1,0:T(8,128)}) %all-gather.2.cloned.1.call-update) | async-done | bytes 1572880 | tf_op jit(solution)/shard_map/all_gather | solution.py:87
  39.5 551.1 %while.58 = (s32[]{:T(128)}, f32[768,2304]{1,0:T(8,128)}, f32[768,768]{1,0:T(8,128)}, f32[768,3072]{1,0:T(8,128)}, f32[3072,768]{1,0:T(8,128)}, /*index=5*/f32[7...) while((s32[]{:T(128)}, f32[768,2304]{1,0:T(8,128)}, ...), condition=%wide.region_26.27_spmd.clone, body=%wide.region_1.26_spmd.clone.sunk | while | flops 34142318592 | bytes 876396608 | solution.py:261
  44.6 11.7 cholesky.217
  56.9 9.8 custom-call.62
  67.3 11.7 cholesky.219
  81.6 4.0 while.59
  85.6 19.7 %custom-call.64 = f32[2,128,128]{1,2,0:T(8,128)S(1)} custom-call(f32[2,128,128]{2,1,0:T(8,128)S(1)} %get-tuple-element.1391), custom_call_target="InvertDiagBlocksLowerTriangular" | custom-call | tf_op jit(solution)/shard_map/while/body/eval_jaxpr/jit(_cho_solve)/triangular_solve | solution.py:55
  117.5 4.4 fusion.298
  129.6 4.1 collective-permute-done
  142.0 4.7 fusion.311
  146.7 4.7 fusion.312
  153.2 6.6 divide_convert_fusion.2
  160.1 7.0 convolution_convert_fusion.5
  168.4 4.9 fusion.315
  173.5 7.2 convert_reduce_fusion.12
  180.7 3.5 multiply_reduce_fusion.8
  191.9 6.3 convert_reduce_fusion.14
  200.0 17.3 %multiply_reduce_fusion.9 = (f32[12,512]{1,0:T(8,128)S(1)}, f32[12,512,768]{2,1,0:T(8,128)}) fusion(f32[12,512,768]{2,1,0:T(8,128)} %copy-done, f32[12,512]{1,0:T(8,128)S(1)} %copy-done.38, pred[512,768]{1,0:T(8,128)(4,1)S(1)} %fusion.295, bf16[512,12,64]{0,2,1:T(8,128)(2,1)S(1)} %bitcast.336, f32[256,12,64]{0,2,1:T(8,128)S(1)} %bitcast.344, ...), kind=kOutput, calls=%fused_computation.4.clone.1 | convolution fusion | flops 629336064 | bytes 41339904 | tf_op jit(solution)/shard_map/while/body/eval_jaxpr/lhd,khd->hlk/dot_general | solution.py:185
  217.3 13.7 %multiply_convert_fusion.11 = bf16[12,512,768]{2,1,0:T(8,128)(2,1)S(1)} fusion(f32[12,512,768]{2,1,0:T(8,128)} %get-tuple-element.1405, f32[12,512,768]{2,1,0:T(8,128)} %copy-done, f32[12,512]{1,0:T(8,128)S(1)} %get-tuple-element.1406, f32[12,512]{1,0:T(8,128)S(1)} %copy-done.38, pred[512,768]{1,0:T(8,128)(4,1)S(1)} %fusion.295), kind=kLoop, calls=%fused_computation.3.clone.1 | loop fusion | flops 28311552 | bytes 47628288 | tf_op jit(solution)/shard_map/while/body/eval_jaxpr/convert_element_type | solution.py:189
  237.1 3.3 fusion.320
  240.5 5.1 fusion.318
  245.7 3.7 select_add_fusion.23
  249.4 10.1 select_add_fusion.25
  266.8 8.2 fusion.324
  275.1 6.0 fusion.319
  281.3 7.1 select_add_fusion.22
  288.7 6.5 select_add_fusion.24
  295.4 3.7 fusion.322
  312.2 11.7 cholesky.217
  324.6 9.8 custom-call.62
  334.9 11.7 cholesky.219
  348.9 4.0 while.59
  352.9 19.7 %custom-call.64 = f32[2,128,128]{1,2,0:T(8,128)S(1)} custom-call(f32[2,128,128]{2,1,0:T(8,128)S(1)} %get-tuple-element.1391), custom_call_target="InvertDiagBlocksLowerTriangular" | custom-call | tf_op jit(solution)/shard_map/while/body/eval_jaxpr/jit(_cho_solve)/triangular_solve | solution.py:55
  381.5 6.5 collective-permute-start
  388.0 4.4 fusion.298
  411.5 4.7 fusion.311
  416.2 4.9 fusion.312
  423.0 6.6 divide_convert_fusion.2
  429.9 7.0 convolution_convert_fusion.5
  438.3 4.9 fusion.315
  443.3 7.2 convert_reduce_fusion.12
  450.5 3.5 multiply_reduce_fusion.8
  461.8 6.3 convert_reduce_fusion.14
  469.8 17.3 %multiply_reduce_fusion.9 = (f32[12,512]{1,0:T(8,128)S(1)}, f32[12,512,768]{2,1,0:T(8,128)}) fusion(f32[12,512,768]{2,1,0:T(8,128)} %copy-done, f32[12,512]{1,0:T(8,128)S(1)} %copy-done.38, pred[512,768]{1,0:T(8,128)(4,1)S(1)} %fusion.295, bf16[512,12,64]{0,2,1:T(8,128)(2,1)S(1)} %bitcast.336, f32[256,12,64]{0,2,1:T(8,128)S(1)} %bitcast.344, ...), kind=kOutput, calls=%fused_computation.4.clone.1 | convolution fusion | flops 629336064 | bytes 41339904 | tf_op jit(solution)/shard_map/while/body/eval_jaxpr/lhd,khd->hlk/dot_general | solution.py:185
  487.1 13.8 %multiply_convert_fusion.11 = bf16[12,512,768]{2,1,0:T(8,128)(2,1)S(1)} fusion(f32[12,512,768]{2,1,0:T(8,128)} %get-tuple-element.1405, f32[12,512,768]{2,1,0:T(8,128)} %copy-done, f32[12,512]{1,0:T(8,128)S(1)} %get-tuple-element.1406, f32[12,512]{1,0:T(8,128)S(1)} %copy-done.38, pred[512,768]{1,0:T(8,128)(4,1)S(1)} %fusion.295), kind=kLoop, calls=%fused_computation.3.clone.1 | loop fusion | flops 28311552 | bytes 47628288 | tf_op jit(solution)/shard_map/while/body/eval_jaxpr/convert_element_type | solution.py:189
  510.3 5.1 fusion.318
  515.6 4.5 select_add_fusion.23
  520.0 13.1 %select_add_fusion.25 = f32[3072,768]{1,0:T(8,128)} fusion(f32[3072,768]{1,0:T(8,128)} %get-tuple-element.1496, pred[]{:T(512)S(6)} %compare.74, bf16[2,512,768]{2,1,0:T(8,128)(2,1)S(1)} %copy-done.28, s32[]{:T(128)S(6)} %copy.104, f32[512,3072]{1,0:T(8,128)} %copy-done.103, f32[3072]{0:T(1024)S(1)} %copy-done.95), kind=kOutput, calls=%fused_computation.11.clone.1 | convolution fusion | flops 2436366336 | bytes 25964548 | tf_op jit(solution)/shard_map/while/body/eval_jaxpr/lf,ld->fd/dot_general | solution.py:166
  540.5 8.2 fusion.324
  548.8 6.0 fusion.319
  555.0 9.1 select_add_fusion.22
  564.4 6.5 select_add_fusion.24
  571.1 3.7 fusion.322
  599.3 5.6 reshape.396
  604.9 10.7 reshape.398
  615.5 10.7 reshape.399
  626.2 7.2 constant_dynamic-update-slice_fusion.5
  635.0 5.0 constant_dynamic-update-slice_fusion.3
  641.3 3.9 constant_dynamic-update-slice_fusion.2
  659.2 489.1 %all-reduce.7.cloned.1.call-done = f32[16,442944]{1,0:T(8,128)} async-done(((f32[16,442944]{1,0:T(8,128)}), f32[16,442944]{1,0:T(8,128)}) %all-reduce.7.cloned.1.call-update) | async-done | bytes 28348432
  1148.3 7.5 constant_dynamic-slice_fusion.2
  1156.4 55.2 %all-reduce.5.cloned.1.call-done = f32[1,442944]{1,0:T(1,128)} async-done(((f32[1,442944]{1,0:T(1,128)}), f32[1,442944]{1,0:T(1,128)}) %all-reduce.5.cloned.1.call-update) | async-done | bytes 1771792 | tf_op jit(solution)/shard_map/psum | solution.py:268
  1213.6 7.2 slice_reduce_fusion
  1228.3 12.5 reduce-scatter.2.cloned.1.call-done
  (683 shorter events, 188.0 us)
Async XLA Ops:
  7.2 32.3 %all-gather.2.cloned.1.call-start = ((), (), s32[]{:S(2)}) async-start(), calls=%async_computation.1 | async-start | bytes 2359296 | tf_op jit(solution)/shard_map/all_gather | solution.py:87
  7.9 1140.4 %all-reduce.7.cloned.1.call-start = ((), (), s32[]{:S(2)}) async-start(), calls=%async_computation.4 | async-start | bytes 56705024
  39.5 90.0 %copy-start.86 = (pred[768]{0:T(1024)(128)(4,1)}, pred[768]{0:T(1024)(128)(4,1)S(1)}, u32[]{:S(2)}) copy-start(pred[768]{0:T(1024)(128)(4,1)S(1)} %get-tuple-element.1571) | copy-start | bytes 2308 | tf_op jit(solution)/shard_map/while
  43.0 24.3 %copy-start.55 = (f32[512]{0:T(512)}, f32[512]{0:T(512)S(1)}, u32[]{:S(2)}) copy-start(f32[512]{0:T(512)S(1)} %fusion.296) | copy-start | bytes 6148 | tf_op jit(solution)/shard_map/while
  43.0 74.5 %copy-start.49 = (f32[512]{0:T(512)}, f32[512]{0:T(512)S(1)}, u32[]{:S(2)}) copy-start(f32[512]{0:T(512)S(1)} %fusion.297) | copy-start | bytes 6148 | tf_op jit(solution)/shard_map/while
  114.2 19.5 %collective-permute-start = (f32[256,768]{1,0:T(8,128)}, f32[256,768]{1,0:T(8,128)}, u32[]{:S(2)}, u32[]{:S(2)}) collective-permute-start(f32[256,768]{1,0:T(8,128)} %convolution_add_fusion.6), channel_id=1, source_target_pairs={{0,1},{2,3},{4,5},{6,7},{8,9},{10,11},{12,13},{14,15},{16,17},{18,... | collective-permute-start | bytes 2359304 | tf_op jit(solution)/shard_map/while/body/eval_jaxpr/while/body/eval_jaxpr/ppermute | solution.py:25
  127.0 15.0 %copy-start.8 = (bf16[512,768]{0,1:T(8,128)(2,1)}, bf16[512,768]{0,1:T(8,128)(2,1)S(1)}, u32[]{:S(2)}) copy-start(bf16[512,768]{0,1:T(8,128)(2,1)S(1)} %copy.67) | copy-start | bytes 2359300 | tf_op jit(solution)/shard_map/while
  127.3 14.7 %copy-start.12 = (bf16[512,768]{0,1:T(8,128)(2,1)}, bf16[512,768]{0,1:T(8,128)(2,1)S(1)}, u32[]{:S(2)}) copy-start(bf16[512,768]{0,1:T(8,128)(2,1)S(1)} %copy.70) | copy-start | bytes 2359300 | tf_op jit(solution)/shard_map/while
  168.1 16.2 %copy-start.46 = (f32[512]{0:T(512)}, f32[512]{0:T(512)S(1)}, u32[]{:S(2)}) copy-start(f32[512]{0:T(512)S(1)} %broadcast_multiply_fusion.9) | copy-start | bytes 6148 | tf_op jit(solution)/shard_map/while
  168.4 15.9 %copy-start.51 = (f32[512]{0:T(512)}, f32[512]{0:T(512)S(1)}, u32[]{:S(2)}) copy-start(f32[512]{0:T(512)S(1)} %fusion.314) | copy-start | bytes 6148 | tf_op jit(solution)/shard_map/while
  168.4 12.2 slice-start.8
  217.3 13.7 %copy-start.13 = (bf16[512,768]{0,1:T(8,128)(2,1)S(1)}, bf16[512,768]{0,1:T(8,128)(2,1)}, u32[]{:S(2)}) copy-start(bf16[512,768]{0,1:T(8,128)(2,1)} %copy-done.12) | copy-start | bytes 2359300 | tf_op jit(solution)/shard_map/while
  217.3 13.7 %copy-start.18 = (bf16[256,768]{0,1:T(8,128)(2,1)S(1)}, bf16[256,768]{0,1:T(8,128)(2,1)}, u32[]{:S(2)}) copy-start(bf16[256,768]{0,1:T(8,128)(2,1)} %copy.69) | copy-start | bytes 1179652 | tf_op jit(solution)/shard_map/while
  265.5 29.9 %collective-permute-start.1 = (f32[256,768]{1,0:T(8,128)}, f32[256,768]{1,0:T(8,128)}, u32[]{:S(2)}, u32[]{:S(2)}) collective-permute-start(f32[256,768]{1,0:T(8,128)} %convolution_add_fusion.7), channel_id=1, source_target_pairs={{1,0},{3,2},{5,4},{7,6},{9,8},{11,10},{13,12},{15,14},{17,16},{19,... | collective-permute-start | bytes 2359304 | tf_op jit(solution)/shard_map/while/body/eval_jaxpr/while/body/eval_jaxpr/ppermute | solution.py:25
  266.8 8.3 copy-start.57
  266.8 8.3 copy-start.61
  266.8 8.3 copy-start.32
  266.8 8.3 copy-start.33
  266.8 8.3 copy-start.35
  281.2 7.5 slice-start
  281.3 7.4 slice-start.1
  281.3 7.4 slice-start.2
  281.3 7.4 copy-start.43
  281.3 7.4 copy-start.47
  281.3 7.4 copy-start.52
  295.3 10.3 copy-start.1
  307.1 92.9 %copy-start.86 = (pred[768]{0:T(1024)(128)(4,1)}, pred[768]{0:T(1024)(128)(4,1)S(1)}, u32[]{:S(2)}) copy-start(pred[768]{0:T(1024)(128)(4,1)S(1)} %get-tuple-element.1571) | copy-start | bytes 2308 | tf_op jit(solution)/shard_map/while
  310.6 24.3 %copy-start.55 = (f32[512]{0:T(512)}, f32[512]{0:T(512)S(1)}, u32[]{:S(2)}) copy-start(f32[512]{0:T(512)S(1)} %fusion.296) | copy-start | bytes 6148 | tf_op jit(solution)/shard_map/while
  310.6 77.4 %copy-start.49 = (f32[512]{0:T(512)}, f32[512]{0:T(512)S(1)}, u32[]{:S(2)}) copy-start(f32[512]{0:T(512)S(1)} %fusion.297) | copy-start | bytes 6148 | tf_op jit(solution)/shard_map/while
  377.8 10.2 copy-start.88
  381.5 21.6 %collective-permute-start = (f32[256,768]{1,0:T(8,128)}, f32[256,768]{1,0:T(8,128)}, u32[]{:S(2)}, u32[]{:S(2)}) collective-permute-start(f32[256,768]{1,0:T(8,128)} %convolution_add_fusion.6), channel_id=1, source_target_pairs={{0,1},{2,3},{4,5},{6,7},{8,9},{10,11},{12,13},{14,15},{16,17},{18,... | collective-permute-start | bytes 2359304 | tf_op jit(solution)/shard_map/while/body/eval_jaxpr/while/body/eval_jaxpr/ppermute | solution.py:25
  397.5 13.9 %copy-start.8 = (bf16[512,768]{0,1:T(8,128)(2,1)}, bf16[512,768]{0,1:T(8,128)(2,1)S(1)}, u32[]{:S(2)}) copy-start(bf16[512,768]{0,1:T(8,128)(2,1)S(1)} %copy.67) | copy-start | bytes 2359300 | tf_op jit(solution)/shard_map/while
  397.8 13.6 %copy-start.12 = (bf16[512,768]{0,1:T(8,128)(2,1)}, bf16[512,768]{0,1:T(8,128)(2,1)S(1)}, u32[]{:S(2)}) copy-start(bf16[512,768]{0,1:T(8,128)(2,1)S(1)} %copy.70) | copy-start | bytes 2359300 | tf_op jit(solution)/shard_map/while
  437.9 16.2 %copy-start.46 = (f32[512]{0:T(512)}, f32[512]{0:T(512)S(1)}, u32[]{:S(2)}) copy-start(f32[512]{0:T(512)S(1)} %broadcast_multiply_fusion.9) | copy-start | bytes 6148 | tf_op jit(solution)/shard_map/while
  438.2 15.9 %copy-start.51 = (f32[512]{0:T(512)}, f32[512]{0:T(512)S(1)}, u32[]{:S(2)}) copy-start(f32[512]{0:T(512)S(1)} %fusion.314) | copy-start | bytes 6148 | tf_op jit(solution)/shard_map/while
  438.3 12.2 slice-start.8
  487.1 13.8 %copy-start.13 = (bf16[512,768]{0,1:T(8,128)(2,1)S(1)}, bf16[512,768]{0,1:T(8,128)(2,1)}, u32[]{:S(2)}) copy-start(bf16[512,768]{0,1:T(8,128)(2,1)} %copy-done.12) | copy-start | bytes 2359300 | tf_op jit(solution)/shard_map/while
  487.1 13.8 %copy-start.18 = (bf16[256,768]{0,1:T(8,128)(2,1)S(1)}, bf16[256,768]{0,1:T(8,128)(2,1)}, u32[]{:S(2)}) copy-start(bf16[256,768]{0,1:T(8,128)(2,1)} %copy.69) | copy-start | bytes 1179652 | tf_op jit(solution)/shard_map/while
  539.1 31.9 %collective-permute-start.1 = (f32[256,768]{1,0:T(8,128)}, f32[256,768]{1,0:T(8,128)}, u32[]{:S(2)}, u32[]{:S(2)}) collective-permute-start(f32[256,768]{1,0:T(8,128)} %convolution_add_fusion.7), channel_id=1, source_target_pairs={{1,0},{3,2},{5,4},{7,6},{9,8},{11,10},{13,12},{15,14},{17,16},{19,... | collective-permute-start | bytes 2359304 | tf_op jit(solution)/shard_map/while/body/eval_jaxpr/while/body/eval_jaxpr/ppermute | solution.py:25
  540.4 8.3 copy-start.57
  540.5 8.3 copy-start.61
  540.5 8.3 copy-start.32
  540.5 8.3 copy-start.33
  540.5 8.3 copy-start.35
  554.8 9.5 slice-start
  554.8 9.3 copy-start.62
  554.8 9.3 copy-start.64
  554.8 9.3 copy-start.82
  554.8 9.3 copy-start.83
  554.9 9.3 copy-start.59
  554.9 9.3 copy-start.60
  554.9 9.3 copy-start.70
  554.9 9.3 copy-start.72
  554.9 9.3 copy-start.74
  554.9 9.3 copy-start.76
  554.9 9.4 slice-start.1
  554.9 9.4 slice-start.2
  554.9 9.4 copy-start.43
  554.9 9.4 copy-start.47
  555.0 9.4 copy-start.52
  571.0 10.3 copy-start.1
  626.2 8.8 copy-start.36
  658.0 553.6 %all-reduce.5.cloned.1.call-start = ((), (), s32[]{:S(2)}) async-start(), calls=%async_computation.3 | async-start | bytes 3544064 | tf_op jit(solution)/shard_map/psum | solution.py:268
  1155.8 84.9 %reduce-scatter.2.cloned.1.call-start = ((), (), s32[]{:S(2)}) async-start(), calls=%async_computation.2 | async-start | bytes 2359296 | tf_op jit(solution)/shard_map/reduce_scatter | solution.py:264
  (167 other events, 726.0 us)
Sparse Core Ops, SparseCore 0:
  9.6 29.8 all-gather.1
  658.1 490.1 all-reduce.6
  1156.0 55.5 all-reduce.4
  1214.4 26.3 reduce-scatter.1
where the time goes:
time: 1250 us
  waiting for transfers between devices  594 us (48%)
  matrix products  262 us (21%)
  other arithmetic  205 us (16%)
  local copies, waits for them, and re-layouts  145 us (12%)
  loops' own time  14.2 us (1%)
  between operations  14.2 us (1%)
  starting transfers between devices  12.5 us (1%)
    unnamed x5, waiting for transfers between devices  490 us
    another operation x14, other arithmetic, memory_maps(): factor = jnp.linalg.cholesky(gram)  69.9 us
    psum x1, waiting for transfers between devices, shards(): summed = lax.psum(summed, 'seg')  55.2 us
    unnamed x25, local copies, waits for them, and re-layouts  39.8 us
    another operation x6, other arithmetic, memory_maps(): solved = jax.scipy.linalg.cho_solve((factor, True), design)  39.4 us
    reshape x13, local copies, waits for them, and re-layouts, shards(): stacked = jnp.concatenate([g.reshape(batch_count, -1) for g in totals], 1)  35.6 us
    dot_general x2, matrix products, micro(): jnp.einsum('lhd,khd->hlk', mixed_heads, value_heads, preferred_element_ty...  34.7 us
    all_gather x1, waiting for transfers between devices, shards(): full_start = lax.all_gather(start_memory, 'seg', axis=2, tiled=True)  29.4 us
  transfers between devices with their start and end apart: 8, of which 6 were waited for; matrix products, arithmetic and copies ran while one was open for 8% of the time, Pallas kernels for 0%

commit v1 on v0

v1 whole, which is shorter than its diff:
```python
import math

import jax
import jax.numpy as jnp
from jax import lax
from jax.sharding import PartitionSpec as P

HEADS = 12
HD = 64
NB = 256
L = 512
STICKY = 512
GRID = 4096

EPSILON = 1e-05
RIDGE = 0.5
MASKED = -1e30
PRECISE = lax.Precision.HIGHEST
F32 = jnp.float32
BF16 = jnp.bfloat16


def shifted_2(block, axis, distance):
    devices = range(lax.axis_size(axis))
    route = [(i - distance, i) for i in devices if i - distance in devices]
    return lax.ppermute(block, axis, route)


def precise(left, right):
    return jnp.matmul(left, right, precision=PRECISE)


def layer_norm(values, gain, offset):
    center = jnp.mean(values, -1, keepdims=True)
    shifted = values - center
    spread = jnp.mean(shifted * shifted, -1, keepdims=True)
    return shifted * lax.rsqrt(spread + EPSILON) * gain + offset


def gelu_tanh(values):
    return jax.nn.gelu(values, approximate=True)


def basis_at(points):
    centers = (jnp.arange(NB, dtype=jnp.float32) + 0.5) / NB
    scaled = (points[None, :] - centers[:, None]) * NB
    return jnp.exp(-0.5 * scaled * scaled)


def memory_maps(positions):
    old_times = (positions.astype(jnp.float32) + 0.5) / GRID
    new_times = 0.5 + 0.5 * (jnp.arange(L, dtype=jnp.float32) + 0.5) / L
    design = jnp.concatenate([basis_at(0.5 * old_times), basis_at(new_times)], axis=1)
    gram = precise(design, design.T) + RIDGE * jnp.eye(NB, dtype=jnp.float32)
    factor = jnp.linalg.cholesky(gram)
    solved = jax.scipy.linalg.cho_solve((factor, True), design)
    carry_map = precise(solved[:, :STICKY], basis_at(old_times).T)
    return (carry_map, solved[:, STICKY:])


def visible():
    row_ids = jnp.arange(L)[:, None]
    col_ids = jnp.arange(L + NB)[None, :]
    return (col_ids >= L) | (col_ids <= row_ids)


def mm(a, b):
    return jnp.dot(a, b, preferred_element_type=F32)


def outer(a, b):
    return lax.dot_general(a, b, (((0,), (0,)), ((), ())), preferred_element_type=F32)


def swap(block, axis, distance):
    n = lax.axis_size(axis)
    return lax.ppermute(block, axis, [(i, i ^ distance) for i in range(n)])


def halve(block, axis, distance, dim):
    bit = (lax.axis_index(axis) // distance) % 2
    send = lax.dynamic_index_in_dim(block, 1 - bit, dim, keepdims=False)
    keep = lax.dynamic_index_in_dim(block, bit, dim, keepdims=False)
    return keep + swap(send, axis, distance)


def spread(grad, seg_place):
    n, s = lax.axis_size("batch"), lax.axis_size("seg")
    bits = n.bit_length() - 1
    rows, cols = grad.shape
    own = rows // n
    split = s if seg_place < bits and own % s == 0 else 1
    work = grad.reshape((2,) * bits + (split, own // split, cols))
    for k in range(bits + 1):
        if k == seg_place:
            if split == 1:
                d = 1
                while d < s:
                    work = work + swap(work, "seg", d)
                    d *= 2
            else:
                left = bits - k
                work = work.reshape((2,) * left + (2,) * (s.bit_length() - 1) + (own // split, cols))
                d = 1
                while d < s:
                    work = halve(work, "seg", d, work.ndim - 3)
                    d *= 2
        if k < bits:
            work = halve(work, "batch", 1 << k, bits - 1 - k)
    if split > 1:
        d = s // 2
        while d >= 1:
            bit = (lax.axis_index("seg") // d) % 2
            other = swap(work, "seg", d)
            work = jnp.where(bit == 0, jnp.concatenate([work, other], 0), jnp.concatenate([other, work], 0))
            d //= 2
    return work.reshape(own, cols)


def shards(
    tokens,
    start_memory,
    has_memory,
    sticky,
    w_qkv,
    w_out,
    w_in,
    w_back,
    q_bias,
    v_bias,
    out_bias,
    in_bias,
    back_bias,
    ln1_gain,
    ln1_bias,
    ln2_gain,
    ln2_bias,
    cotangent,
):
    width = w_qkv.shape[0]
    docs = tokens.shape[0]
    scale = HD ** (-0.5)
    is_first = lax.axis_index("seg") == 0
    chain = lax.axis_size("seg")
    flags = has_memory.astype(F32)[:, None, None]
    allowed = visible()

    full_start = lax.all_gather(start_memory, "seg", axis=2, tiled=True)
    own_start = jnp.where(is_first, flags * full_start, 0.0)

    x = tokens[:, 0].astype(F32)
    cot = cotangent[:, 0].reshape(docs * L, width)
    carry_map, data_map = jax.vmap(memory_maps)(sticky[:, 0])
    hidden = layer_norm(x, ln1_gain, ln1_bias).astype(BF16)
    fresh = precise(data_map, hidden.astype(F32))

    def down_step(_, incoming):
        return shifted_2(precise(carry_map, incoming) + fresh, "seg", 1) + own_start

    memory = own_start
    for i in range(chain - 1):
        memory = down_step(i, memory)

    hidden_rows = hidden.reshape(docs * L, width)
    projected = mm(hidden_rows, w_qkv)
    act_grad = mm(cot, w_back.T)
    mem_in = memory.astype(BF16)
    mem_rows = mem_in.reshape(docs * NB, width)
    mem_proj = mm(mem_rows, w_qkv[:, width:]).reshape(docs, NB, 2 * width)
    projected = projected.reshape(docs, L, 3 * width)
    query = (projected[..., :width] + q_bias).astype(BF16)
    keys = jnp.concatenate([projected[..., width : 2 * width], mem_proj[..., :width]], 1).astype(BF16)
    values = (jnp.concatenate([projected[..., 2 * width :], mem_proj[..., width:]], 1) + v_bias).astype(BF16)
    qh = query.reshape(docs, L, HEADS, HD)
    kh = keys.reshape(docs, L + NB, HEADS, HD)
    vh = values.reshape(docs, L + NB, HEADS, HD)

    def scores_of():
        s = jnp.einsum("blhd,bkhd->bhlk", qh, kh, preferred_element_type=F32) * scale
        return jnp.where(allowed[None, None], s, MASKED)

    scores = scores_of()
    peak = jnp.max(scores, -1, keepdims=True)
    weight = jnp.exp(scores - peak)
    total = jnp.sum(weight, -1, keepdims=True)
    log_total = peak + jnp.log(total)
    probs = (weight / total).astype(BF16)
    mixed = jnp.einsum("bhlk,bkhd->blhd", probs, vh, preferred_element_type=F32).astype(BF16)
    mixed = mixed.reshape(docs * L, width)
    x_rows = x.reshape(docs * L, width)
    residual = x_rows + (mm(mixed, w_out) + out_bias)
    normed = layer_norm(residual, ln2_gain, ln2_bias).astype(BF16)
    pre_act = mm(normed, w_in) + in_bias
    activated, gelu_back = jax.vjp(gelu_tanh, pre_act)
    act_low = activated.astype(BF16)
    grad_back = spread(outer(act_low, cot), 2)
    output = (residual + (mm(act_low, w_back) + back_bias)).astype(BF16)
    out_grad = cot.astype(F32)
    (pre_grad,) = gelu_back(act_grad)
    pre_low = pre_grad.astype(BF16)
    grad_in = spread(outer(normed, pre_low), 1)
    normed_grad = mm(pre_low, w_in.T)
    _, norm_two_back = jax.vjp(layer_norm, residual, ln2_gain, ln2_bias)
    residual_part, gain_two, bias_two = norm_two_back(normed_grad)
    residual_grad = out_grad + residual_part
    branch = residual_grad.astype(BF16)
    grad_out = spread(outer(mixed, branch), 2)
    mixed_grad = mm(branch, w_out.T).astype(BF16)
    mh = mixed_grad.reshape(docs, L, HEADS, HD)
    chances = jnp.exp(scores_of() - log_total)
    prob_grad = jnp.einsum("blhd,bkhd->bhlk", mh, vh, preferred_element_type=F32)
    delta = jnp.sum(chances * prob_grad, -1, keepdims=True)
    score_low = (chances * (prob_grad - delta)).astype(BF16)
    query_grad = (jnp.einsum("bhlk,bkhd->blhd", score_low, kh, preferred_element_type=F32) * scale).astype(BF16)
    key_grad = (jnp.einsum("bhlk,blhd->bkhd", score_low, qh, preferred_element_type=F32) * scale).astype(BF16)
    value_grad = jnp.einsum("bhlk,blhd->bkhd", probs, mh, preferred_element_type=F32).astype(BF16)
    query_grad = query_grad.reshape(docs, L, width)
    key_grad = key_grad.reshape(docs, L + NB, width)
    value_grad = value_grad.reshape(docs, L + NB, width)
    token_proj = jnp.concatenate([query_grad, key_grad[:, :L], value_grad[:, :L]], 2).reshape(docs * L, 3 * width)
    memory_proj = jnp.concatenate([key_grad[:, L:], value_grad[:, L:]], 2).reshape(docs * NB, 2 * width)
    local_grad = mm(memory_proj, w_qkv[:, width:].T).reshape(docs, NB, width)
    carry_back = carry_map.swapaxes(1, 2)
    incoming = jnp.zeros_like(local_grad)
    for i in range(chain - 1):
        incoming = shifted_2(precise(carry_back, incoming) + local_grad, "seg", -1)
    key_rows = token_proj[:, width : 2 * width]
    value_rows = token_proj[:, 2 * width :]
    grad_q = spread(outer(hidden_rows, token_proj[:, :width]), 1)
    grad_k = spread(outer(hidden_rows, key_rows) + outer(mem_rows, memory_proj[:, :width]), 2)
    grad_v = spread(outer(hidden_rows, value_rows) + outer(mem_rows, memory_proj[:, width:]), 1)
    hidden_grad = mm(token_proj, w_qkv.T)
    hidden_grad = hidden_grad + precise(data_map.swapaxes(1, 2), incoming).reshape(docs * L, width)
    _, norm_one_back = jax.vjp(layer_norm, x_rows, ln1_gain, ln1_bias)
    token_part, gain_one, bias_one = norm_one_back(hidden_grad)
    input_grad = (residual_grad + token_part).astype(BF16)
    start_grad = jnp.where(is_first, flags * (local_grad + precise(carry_back, incoming)), 0.0)
    start_share = lax.psum_scatter(start_grad, "seg", scatter_dimension=2, tiled=True)

    batch = lax.axis_size("batch")
    small = [
        jnp.sum(query_grad.astype(F32), (0, 1)),
        jnp.sum(value_grad.astype(F32), (0, 1)),
        jnp.sum(branch.astype(F32), 0),
        jnp.sum(pre_low.astype(F32), 0),
        jnp.sum(out_grad, 0),
        gain_one,
        bias_one,
        gain_two,
        bias_two,
    ]
    packed = jnp.concatenate([g.reshape(batch, -1) for g in small], 1)
    packed = spread(packed, 4)[0]
    vectors = []
    offset = 0
    for g in small:
        length = g.shape[0] // batch
        vectors.append(packed[offset : offset + length])
        offset += length
    grad_qkv = jnp.concatenate([grad_q, grad_k, grad_v], 1)
    return (
        output.reshape(docs, 1, L, width),
        input_grad.reshape(docs, 1, L, width),
        start_share,
        grad_qkv,
        grad_out,
        grad_in,
        grad_back,
    ) + tuple(vectors)


def solution(mesh):
    rows = P("batch", "seg", None, None)
    in_specs = (rows, P("batch", None, "seg"), P("batch"), P("batch", "seg", None)) + (P(),) * 13 + (rows,)
    out_specs = (rows, rows, P("batch", None, "seg")) + (P("batch", None),) * 4 + (P("batch"),) * 9
    return jax.shard_map(shards, mesh=mesh, in_specs=in_specs, out_specs=out_specs, check_vma=False)
```

time: 1250 us -> 763 us (0.61)
  waiting for transfers between devices: 594 us -> 156 us
  local copies, waits for them, and re-layouts: 145 us -> 94.4 us
  matrix products: 262 us -> 213 us
  starting transfers between devices: 12.5 us -> 45.3 us
  other arithmetic: 205 us -> 232 us
  loops' own time: 14.2 us -> 0.01 us
    unnamed x5 -> x2, waiting for transfers between devices: 490 us -> 0.7 us
    ppermute x0 -> x41, waiting for transfers between devices: none -> 140 us  [swap(): return lax.ppermute(block, axis, [(i, i ^ distance) for i in range(n)])]
    psum x1 -> x0, waiting for transfers between devices: 55.2 us -> none  [shards(): summed = lax.psum(summed, 'seg')]
    dot_general x56 -> x31, matrix products: 254 us -> 203 us  [the longest x10 67.6 us: mm(): return jnp.dot(a, b, preferred_element_type=F32)]
    ppermute x0 -> x41, starting transfers between devices: none -> 37.5 us  [swap(): return lax.ppermute(block, axis, [(i, i ^ distance) for i in range(n)])]
    reshape x17 -> x1, local copies, waits for them, and re-layouts: 39 us -> 3.28 us  [shards(): mh = mixed_grad.reshape(docs, L, HEADS, HD)]
    all_gather x1, waiting for transfers between devices: 29.4 us -> 0.02 us  [shards(): full_start = lax.all_gather(start_memory, 'seg', axis=2, tiled=True)]
    unnamed x25 -> x201, local copies, waits for them, and re-layouts: 39.8 us -> 15.6 us
  transfers between devices with their start and end apart: 8 -> 45, of which waited for: 6 -> 17; matrix products, arithmetic and copies ran while one was open for 8% -> 36% of each run, Pallas kernels for 0% -> 0%
where the time goes in v1:
time: 763 us; the launch traced here: 758 us
  other arithmetic  232 us (30%)
  matrix products  213 us (28%)
  waiting for transfers between devices  156 us (20%)
  local copies, waits for them, and re-layouts  94.4 us (12%)
  starting transfers between devices  45.3 us (6%)
  between operations  16.3 us (2%)
    ppermute x41, waiting for transfers between devices, swap(): return lax.ppermute(block, axis, [(i, i ^ distance) for i in range(n)])  140 us
    another operation x10, other arithmetic, memory_maps(): factor = jnp.linalg.cholesky(gram)  71.5 us
    dot_general x10, matrix products, mm(): return jnp.dot(a, b, preferred_element_type=F32)  67.6 us
    another operation x4, other arithmetic, memory_maps(): solved = jax.scipy.linalg.cho_solve((factor, True), design)  42.7 us
    ppermute x41, starting transfers between devices, swap(): return lax.ppermute(block, axis, [(i, i ^ distance) for i in range(n)])  37.5 us
    convert_element_type x1, other arithmetic, shards(): score_low = (chances * (prob_grad - delta)).astype(BF16)  30.6 us
    dot_general x1, matrix products, shards(): jnp.einsum('blhd,bkhd->bhlk', mh, vh, preferred_element_type=F32)  28.9 us
    dot_general x8, matrix products, outer(): lax.dot_general(a, b, (((0,), (0,)), ((), ())), preferred_element_type=F32)  25.1 us
  transfers between devices with their start and end apart: 45, of which 17 were waited for; matrix products, arithmetic and copies ran while one was open for 36% of the time, Pallas kernels for 0%

profile of v1, /device:TPU:0, one launch (start us, length us, event | category | flops | bytes accessed | tf_op | source)
XLA Modules:
  0.0 757.7 jit_solution(16358826250039491011)
XLA Ops:
  25.7 23.9 %custom-call.20 = f32[2,128,128]{2,1,0:T(8,128)S(1)} custom-call(f32[2,128,128]{2,1,0:T(8,128)S(1)} %cholesky.122), custom_call_target="Cholesky" | custom-call | tf_op jit(solution)/shard_map/vmap(jit(cholesky))/cholesky | solution.py:55
  50.4 20.3 %custom-call.21 = f32[2,1,128,128]{2,3,1,0:T(8,128)} custom-call(f32[2,1,128,128]{3,2,1,0:T(8,128)S(1)} %select_bitcast_fusion), custom_call_target="InvertDiagBlocksLowerTriangular" | custom-call | tf_op jit(solution)/shard_map/vmap(jit(cholesky))/cholesky | solution.py:55
  73.9 24.3 %custom-call.22 = f32[2,128,128]{2,1,0:T(8,128)S(1)} custom-call(f32[2,128,128]{2,1,0:T(8,128)} %convolution_subtract_fusion.2), custom_call_target="Cholesky" | custom-call | tf_op jit(solution)/shard_map/vmap(jit(cholesky))/cholesky | solution.py:55
  101.7 5.3 while.1
  107.0 40.3 %custom-call.23 = f32[2,2,128,128]{2,3,1,0:T(8,128)S(1)} custom-call(f32[2,2,128,128]{3,2,1,0:T(8,128)} %bitcast.444), custom_call_target="InvertDiagBlocksLowerTriangular" | custom-call | tf_op jit(solution)/shard_map/vmap(jit(_cho_solve))/triangular_solve | solution.py:56
  147.3 2.4 fusion.79
  160.1 3.2 fusion.66
  163.4 3.1 convolution_add_fusion.3
  166.5 6.4 collective-permute-start
  172.9 4.2 fusion.25
  178.4 2.6 fusion.152
  181.0 3.6 copy.101
  184.6 2.6 copy.111
  187.2 2.6 copy.110
  189.9 15.4 %collective-permute-done = f32[2,256,768]{2,1,0:T(8,128)} collective-permute-done((f32[2,256,768]{2,1,0:T(8,128)}, f32[2,256,768]{2,1,0:T(8,128)}, u32[]{:S(2)}, u32[]{:S(2)}) %collective-permute-start) | collective-permute-done | bytes 1572896 | tf_op jit(solution)/shard_map/ppermute | solution.py:26
  211.1 2.3 copy.112
  213.5 18.5 %fusion.1 = (f32[2,12,512]{2,1,0:T(8,128)S(1)}, f32[2,12,512,768]{3,2,1,0:T(8,128)}) fusion(pred[512,768]{1,0:T(8,128)(4,1)S(1)} %fusion.62, bf16[2,512,12,64]{1,3,2,0:T(8,128)(2,1)} %bitcast.390, bf16[2,256,12,64]{1,3,2,0:T(8,128)(2,1)} %bitcast.408, bf16[2,512,12,64]{1,3,2,0:T(8,128)(2,1)} %bitcast.398), kind=kOutput, calls=%fused_computation.9 | convolution fusion | flops 1240977408 | bytes 42123264 | tf_op jit(solution)/shard_map/blhd,bkhd->bhlk/dot_general | solution.py:179
  232.0 19.5 %fusion = f32[2,12,512]{2,1,0:T(8,128)S(1)} fusion(f32[2,12,512,768]{3,2,1,0:T(8,128)} %get-tuple-element.133, f32[2,12,512]{2,1,0:T(8,128)S(1)} %get-tuple-element.132, pred[512,768]{1,0:T(8,128)(4,1)S(1)} %fusion.62), kind=kLoop, calls=%fused_computation.8 | loop fusion | flops 37736448 | bytes 38240256 | tf_op jit(solution)/shard_map/reduce_sum | solution.py:185
  251.5 22.9 %divide_convert_fusion = bf16[2,12,512,768]{3,2,1,0:T(8,128)(2,1)} fusion(f32[2,12,512,768]{3,2,1,0:T(8,128)} %get-tuple-element.133, f32[2,12,512]{2,1,0:T(8,128)S(1)} %fusion, f32[2,12,512]{2,1,0:T(8,128)S(1)} %get-tuple-element.132, pred[512,768]{1,0:T(8,128)(4,1)S(1)} %fusion.62), kind=kLoop, calls=%fused_computation.5 | loop fusion | flops 47185920 | bytes 57114624 | tf_op jit(solution)/shard_map/convert_element_type | solution.py:187
  274.4 3.0 copy.109
  277.4 12.1 %fusion.65 = bf16[2,512,12,64]{1,3,2,0:T(8,128)(2,1)} fusion(bf16[2,12,512,768]{3,2,1,0:T(8,128)(2,1)} %divide_convert_fusion, f32[2,256,12,64]{1,3,2,0:T(8,128)} %bitcast.394, f32[2,512,12,64]{1,3,2,0:T(8,128)} %bitcast.386, f32[12,64]{1,0:T(8,128)S(1)} %add.533), kind=kOutput, calls=%fused_computation.137 | convolution fusion | flops 1212284928 | bytes 25168896 | tf_op jit(solution)/shard_map/bhlk,bkhd->blhd/dot_general | solution.py:188
  289.5 3.0 copy.113
  296.6 11.2 %fusion.16 = (bf16[3072,1024]{0,1:T(8,128)(2,1)}, f32[1024,3072]{1,0:T(8,128)}) fusion(f32[3072]{0:T(1024)S(1)} %copy-done.82, bf16[768,3072]{1,0:T(8,128)(2,1)S(1)} %bitcast.443, f32[1024,768]{1,0:T(8,128)S(1)} %get-tuple-element.135, f32[768]{0:T(1024)S(1)} %copy-done.55, f32[768]{0:T(1024)S(1)} %copy-done.52, f32[1024]{0:T(1024)S(1)} %fusion.117, ...), kind=kOutput, calls=%fused_computation.27 | convolution fusion | flops 4867227648 | bytes 26765312 | tf_op jit(solution)/shard_map/dot_general | solution.py:68
  307.8 15.8 %convert_reduce_fusion = (f32[3072]{0:T(1024)}, bf16[1024,3072]{1,0:T(8,128)(2,1)S(1)}) fusion(f32[1024,3072]{1,0:T(8,128)} %get-tuple-element.141, f32[3072]{0:T(1024)S(1)} %copy-done.82, bf16[1024,768]{1,0:T(8,128)(2,1)S(1)} %bitcast.396, bf16[3072,768]{1,0:T(8,128)(2,1)} %param.25), kind=kOutput, calls=%fused_computation.28 | convolution fusion | flops 4904186880 | bytes 25190400 | tf_op jit(solution)/shard_map/dot_general | solution.py:68
  323.6 8.6 %multiply_reduce_fusion.1 = (f32[768]{0:T(1024)}, f32[1024]{0:T(1024)S(1)}, f32[768]{0:T(1024)}, f32[1024,768]{1,0:T(8,128)S(1)}) fusion(f32[1024,768]{1,0:T(8,128)S(1)} %get-tuple-element.135, f32[1024]{0:T(1024)S(1)} %fusion.117, f32[1024]{0:T(1024)S(1)} %broadcast_multiply_fusion, f32[768]{0:T(1024)S(1)} %copy-done.52, ...), kind=kOutput, calls=%fused_computation.83 | convolution fusion | flops 4838126592 | bytes 17323008 | tf_op jit(solution)/shard_map/dot_general | solution.py:68
  332.2 8.4 %fusion.146 = f32[768,3072]{1,0:T(8,128)} fusion(bf16[1024,3072]{1,0:T(8,128)(2,1)S(1)} %get-tuple-element.147, f32[1024,768]{1,0:T(8,128)S(1)} %get-tuple-element.135, f32[768]{0:T(1024)S(1)} %copy-done.55, f32[768]{0:T(1024)S(1)} %copy-done.52, f32[1024]{0:T(1024)S(1)} %fusion.117, f32[1024]{0:T(1024)S(1)} %broadcast_multiply_fusion), kind=kOutput, calls=%fused_computation.335 | convolution fusion | flops 4835770368 | bytes 18888704 | tf_op jit(solution)/shard_map/dot_general | solution.py:72
  347.9 3.3 reshape.437
  351.2 9.7 %convert_reduce_fusion.1 = (f32[12,64]{1,0:T(8,128)S(1)}, bf16[2,12,64,768]{3,2,1,0:T(8,128)(2,1)S(1)}) fusion(bf16[2,12,512,768]{3,2,1,0:T(8,128)(2,1)} %divide_convert_fusion, bf16[2,512,12,64]{1,0,3,2:T(2,128)(2,1)S(1)} %reshape.437), kind=kOutput, calls=%fused_computation.44 | convolution fusion | flops 1211497728 | bytes 22809600 | tf_op jit(solution)/shard_map/bhlk,blhd->bkhd/dot_general | solution.py:216
  362.2 28.9 %multiply_reduce_fusion = (f32[2,12,512]{2,1,0:T(8,128)S(1)}, f32[2,12,512,768]{3,2,1,0:T(8,128)}) fusion(f32[2,12,512,768]{3,2,1,0:T(8,128)} %get-tuple-element.133, f32[2,12,512]{2,1,0:T(8,128)S(1)} %log_add_fusion, pred[512,768]{1,0:T(8,128)(4,1)S(1)} %fusion.62, f32[2,256,12,64]{1,3,2,0:T(8,128)} %bitcast.395, f32[2,512,12,64]{1,3,2,0:T(8,128)} %bitcast.387, ...), kind=kOutput, calls=%fused_computation.3 | convolution fusion | flops 1258672128 | bytes 82283520 | tf_op jit(solution)/shard_map/blhd,bkhd->bhlk/dot_general | solution.py:211
  391.1 30.6 %multiply_convert_fusion = bf16[2,12,512,768]{3,2,1,0:T(8,128)(2,1)} fusion(f32[2,12,512,768]{3,2,1,0:T(8,128)} %get-tuple-element.138, f32[2,12,512,768]{3,2,1,0:T(8,128)} %get-tuple-element.133, f32[2,12,512]{2,1,0:T(8,128)S(1)} %get-tuple-element.137, f32[2,12,512]{2,1,0:T(8,128)S(1)} %log_add_fusion, pred[512,768]{1,0:T(8,128)(4,1)S(1)} %fusion.62), kind=kLoop, calls=%fused_computation.2 | loop fusion | flops 56623104 | bytes 94863360 | tf_op jit(solution)/shard_map/convert_element_type | solution.py:213
  421.7 9.6 %multiply_convert_fusion.3 = bf16[2,12,64,768]{3,2,1,0:T(8,128)(2,1)S(1)} fusion(bf16[2,512,12,64]{1,3,2,0:T(8,128)(2,1)S(1)} %bitcast.391, bf16[2,12,512,768]{3,2,1,0:T(8,128)(2,1)} %multiply_convert_fusion), kind=kOutput, calls=%fused_computation.46 | convolution fusion | flops 1210318848 | bytes 22806528 | tf_op jit(solution)/shard_map/bhlk,blhd->bkhd/dot_general | solution.py:215
  433.2 3.1 fusion.50
  437.9 8.7 %copy.137 = bf16[3072,1024]{1,0:T(8,128)(2,1)} copy(bf16[3072,1024]{0,1:T(8,128)(2,1)} %get-tuple-element.140) | data formatting | bytes 12582912 | tf_op jit(solution)/shard_map/convert_element_type | solution.py:195
  446.6 13.7 %add_convert_fusion.1 = bf16[1024,768]{1,0:T(8,128)(2,1)} fusion(f32[1024,768]{1,0:T(8,128)} %copy-done.4, bf16[3072,768]{1,0:T(8,128)(2,1)} %param.25, f32[1024,3072]{1,0:T(8,128)} %get-tuple-element.141, f32[3072]{0:T(1024)S(1)} %copy-done.83, f32[768]{0:T(1024)S(1)} %copy-done.85), kind=kOutput, calls=%fused_computation.91 | convolution fusion | flops 4865654784 | bytes 22035456 | tf_op jit(solution)/shard_map/dot_general | solution.py:68
  475.4 2.6 convolution_add_fusion.2
  479.3 7.8 %fusion.156 = f32[2,2,2,2,2,96,768]{6,5,4,3,2,1,0:T(8,128)} fusion(bf16[2,2,2,2,2,96,1024]{6,5,4,3,2,1,0:T(8,128)(2,1)S(1)} %bitcast.412, bf16[1024,768,1,1,1,1,1]{1,0,6,5,4,3,2:T(8,128)(2,1)S(1)} %bitcast.397), kind=kOutput, calls=%fused_computation.344 | convolution fusion | flops 4831838208 | bytes 17301504 | tf_op jit(solution)/shard_map/dot_general | solution.py:72
  487.1 9.7 %convert_reduce_fusion.5 = (f32[12,64]{1,0:T(8,128)S(1)}, bf16[2,512,12,64]{1,3,2,0:T(8,128)(2,1)S(1)}) fusion(bf16[2,12,512,768]{3,2,1,0:T(8,128)(2,1)} %multiply_convert_fusion, bf16[2,256,12,64]{1,3,2,0:T(8,128)(2,1)S(1)} %bitcast.409, bf16[2,512,12,64]{1,3,2,0:T(8,128)(2,1)S(1)} %bitcast.399), kind=kOutput, calls=%fused_computation.86 | convolution fusion | flops 1215823104 | bytes 22809600 | tf_op jit(solution)/shard_map/bhlk,bkhd->blhd/dot_general | solution.py:214
  496.9 8.5 %constant_dynamic-slice_fusion.10 = (f32[2,2,2,1,2,24,3072]{6,5,4,3,2,1,0:T(8,128)}, f32[2,2,2,1,2,24,3072]{6,5,4,3,2,1,0:T(8,128)}) fusion(f32[2,2,2,2,2,24,3072]{6,5,4,3,2,1,0:T(8,128)} %bitcast.385, s32[]{:T(128)S(6)} %select_n.313, s32[]{:T(128)S(6)} %select_n.314), kind=kLoop, calls=%fused_computation.265 | loop fusion | bytes 18874376 | tf_op jit(solution)/shard_map/jit(dynamic_index_in_dim)/dynamic_slice | solution.py:83
  505.8 5.0 copy.213
  510.8 4.9 dynamic-slice_bitcast_fusion
  525.8 3.8 collective-permute-start.15
  532.1 4.4 fusion.98
  536.6 6.6 fusion.148
  543.3 3.0 fusion.49
  546.8 4.6 multiply_select_fusion.1
  552.1 3.1 collective-permute-done.39
  556.9 5.4 fusion.47
  562.3 2.9 copy.125
  565.2 2.7 collective-permute-start.41
  568.0 3.1 fusion.60
  571.8 3.0 collective-permute-done.42
  579.6 8.7 %collective-permute-done.9 = f32[2,2,2,24,768]{4,3,2,1,0:T(8,128)S(1)} collective-permute-done((f32[2,2,2,24,768]{4,3,2,1,0:T(8,128)S(1)}, f32[2,2,2,24,768]{4,3,2,1,0:T(8,128)S(1)}, u32[]{:S(2)}, u32[]{:S(2)}) %collective-permute-start.9) | collective-permute-done | bytes 589856 | tf_op jit(solution)/shard_map/ppermute | solution.py:77
  589.6 5.5 collective-permute-done.16
  597.3 4.9 collective-permute-done.23
  602.2 2.3 collective-permute-done.17
  607.6 3.1 bitcast_add_fusion
  611.8 3.1 bitcast_add_fusion.1
  623.4 58.7 %collective-permute-done.25 = f32[24,768]{1,0:T(8,128)S(1)} collective-permute-done((f32[24,768]{1,0:T(8,128)S(1)}, f32[24,768]{1,0:T(8,128)S(1)}, u32[]{:S(2)}, u32[]{:S(2)}) %collective-permute-start.25) | collective-permute-done | bytes 73760 | tf_op jit(solution)/shard_map/ppermute | solution.py:77
  691.3 3.7 collective-permute-done.5
  696.5 7.9 %collective-permute-done.34 = f32[2,2,96,768]{3,2,1,0:T(8,128)S(1)} collective-permute-done((f32[2,2,96,768]{3,2,1,0:T(8,128)S(1)}, f32[2,2,96,768]{3,2,1,0:T(8,128)S(1)}, u32[]{:S(2)}, u32[]{:S(2)}) %collective-permute-start.34) | collective-permute-done | bytes 1179680 | tf_op jit(solution)/shard_map/ppermute | solution.py:77
  707.6 12.8 %collective-permute-done.35 = f32[2,96,768]{2,1,0:T(8,128)S(1)} collective-permute-done((f32[2,96,768]{2,1,0:T(8,128)S(1)}, f32[2,96,768]{2,1,0:T(8,128)S(1)}, u32[]{:S(2)}, u32[]{:S(2)}) %collective-permute-start.35) | collective-permute-done | bytes 589856 | tf_op jit(solution)/shard_map/ppermute | solution.py:77
  722.6 10.5 %collective-permute-done.29 = f32[2,24,3072]{2,1,0:T(8,128)S(1)} collective-permute-done((f32[2,24,3072]{2,1,0:T(8,128)S(1)}, f32[2,24,3072]{2,1,0:T(8,128)S(1)}, u32[]{:S(2)}, u32[]{:S(2)}) %collective-permute-start.29) | collective-permute-done | bytes 589856 | tf_op jit(solution)/shard_map/ppermute | solution.py:77
  733.4 9.6 %collective-permute-done.30 = f32[24,3072]{1,0:T(8,128)S(1)} collective-permute-done((f32[24,3072]{1,0:T(8,128)S(1)}, f32[24,3072]{1,0:T(8,128)S(1)}, u32[]{:S(2)}, u32[]{:S(2)}) %collective-permute-start.30) | collective-permute-done | bytes 294944 | tf_op jit(solution)/shard_map/ppermute | solution.py:77
  744.8 5.1 collective-permute-done.31
  (447 shorter events, 137.0 us)
Async XLA Ops:
  7.2 285.8 %copy-start = (bf16[768,768]{1,0:T(8,128)(2,1)S(1)}, bf16[768,768]{1,0:T(8,128)(2,1)}, u32[]{:S(2)}) copy-start(bf16[768,768]{1,0:T(8,128)(2,1)} %param.23) | copy-start | bytes 3538948
  7.2 10.3 %copy-start.74 = (f32[768]{0:T(1024)S(1)}, f32[768]{0:T(1024)}, u32[]{:S(2)}) copy-start(f32[768]{0:T(1024)} %param.27) | copy-start | bytes 9220
  7.2 10.4 %copy-start.75 = (s32[2,1,512]{2,1,0:T(1,128)S(1)}, s32[2,1,512]{2,1,0:T(1,128)}, u32[]{:S(2)}) copy-start(s32[2,1,512]{2,1,0:T(1,128)} %param.21) | copy-start | bytes 12292
  7.2 152.8 %all-gather.2.cloned.1.call-start = ((), (), s32[]{:S(2)}) async-start(), calls=%async_computation.1 | async-start | bytes 2359296 | tf_op jit(solution)/shard_map/all_gather | solution.py:148
  8.0 742.8 %reduce-scatter.2.cloned.1.call-start = ((), (), s32[]{:S(2)}) async-start(), calls=%async_computation.2 | async-start | bytes 2359296 | tf_op jit(solution)/shard_map/reduce_scatter | solution.py:238
  98.2 51.5 %copy-start.53 = (f32[768]{0:T(1024)S(1)}, f32[768]{0:T(1024)}, u32[]{:S(2)}) copy-start(f32[768]{0:T(1024)} %param.31) | copy-start | bytes 9220
  166.5 38.8 %collective-permute-start = (f32[2,256,768]{2,1,0:T(8,128)}, f32[2,256,768]{2,1,0:T(8,128)}, u32[]{:S(2)}, u32[]{:S(2)}) collective-permute-start(f32[2,256,768]{2,1,0:T(8,128)} %convolution_add_fusion.3), channel_id=1, source_target_pairs={{0,1},{2,3},{4,5},{6,7},{8,9},{10,11},{12,13},{14,15},{16,17},{18,... | collective-permute-start | bytes 4718600 | tf_op jit(solution)/shard_map/ppermute | solution.py:26
  184.6 20.8 %copy-start.69 = (f32[2]{0:T(128)S(1)}, f32[2]{0:T(128)}, u32[]{:S(2)}) copy-start(f32[2]{0:T(128)} %convert_element_type.133) | copy-start | bytes 28
  189.8 17.7 %copy-start.80 = (bf16[768,2304]{1,0:T(8,128)(2,1)S(1)}, bf16[768,2304]{1,0:T(8,128)(2,1)}, u32[]{:S(2)}) copy-start(bf16[768,2304]{1,0:T(8,128)(2,1)} %param.22) | copy-start | bytes 10616836
  294.7 45.8 %copy-start.4 = (f32[1024,768]{1,0:T(8,128)}, f32[1024,768]{1,0:T(8,128)S(1)}, u32[]{:S(2)}) copy-start(f32[1024,768]{1,0:T(8,128)S(1)} %get-tuple-element.135) | copy-start | bytes 9437188
  296.5 11.3 %copy-start.14 = (bf16[2,1,512,768]{3,2,1,0:T(8,128)(2,1)S(1)}, bf16[2,1,512,768]{3,2,1,0:T(8,128)(2,1)}, u32[]{:S(2)}) copy-start(bf16[2,1,512,768]{3,2,1,0:T(8,128)(2,1)} %param.35) | copy-start | bytes 4718596
  391.1 30.7 %copy-start.6 = (bf16[2,512,768]{1,2,0:T(8,128)(2,1)S(1)}, bf16[2,512,768]{1,2,0:T(8,128)(2,1)}, u32[]{:S(2)}) copy-start(bf16[2,512,768]{1,2,0:T(8,128)(2,1)} %copy.110) | copy-start | bytes 4718596
  436.3 39.0 %copy-start.23 = (f32[2,256,768]{2,1,0:T(8,128)}, f32[2,256,768]{2,1,0:T(8,128)S(1)}, u32[]{:S(2)}) copy-start(f32[2,256,768]{2,1,0:T(8,128)S(1)} %fusion.50) | copy-start | bytes 4718596
  446.5 13.7 %copy-start.48 = (bf16[96,8,2,512]{3,1,2,0:T(8,128)(2,1)S(1)}, bf16[96,8,2,512]{3,1,2,0:T(8,128)(2,1)}, u32[]{:S(2)}) copy-start(bf16[96,8,2,512]{3,1,2,0:T(8,128)(2,1)} %copy-done.47) | copy-start | bytes 4718596
  446.5 13.7 %copy-start.50 = (bf16[1024,768]{1,0:T(8,128)(2,1)S(1)}, bf16[1024,768]{1,0:T(8,128)(2,1)}, u32[]{:S(2)}) copy-start(bf16[1024,768]{1,0:T(8,128)(2,1)} %copy-done.49) | copy-start | bytes 4718596
  463.1 54.7 %collective-permute-start.20 = (f32[2,2,2,2,24,768]{5,4,3,2,1,0:T(8,128)}, f32[2,2,2,2,24,768]{5,4,3,2,1,0:T(8,128)}, u32[]{:S(2)}, u32[]{:S(2)}) collective-permute-start(f32[2,2,2,2,24,768]{5,4,3,2,1,0:T(8,128)} %dynamic-slice_bitcast_fusion.4), channel_id=1, source_target_pairs={{0,2},{2,0},{4,6},{6,4},{8,10},{10,8},{12,14},{14,12},{16,18},{18,... | collective-permute-start | bytes 3538952 | tf_op jit(solution)/shard_map/ppermute | solution.py:77
  474.9 47.1 %collective-permute-start.14 = (f32[2,2,2,2,24,768]{5,4,2,1,0,3:T(8,128)}, f32[2,2,2,2,24,768]{5,4,2,1,0,3:T(8,128)}, u32[]{:S(2)}, u32[]{:S(2)}) collective-permute-start(f32[2,2,2,2,24,768]{5,4,2,1,0,3:T(8,128)} %bitcast.373), channel_id=1, source_target_pairs={{0,2},{2,0},{4,6},{6,4},{8,10},{10,8},{12,14},{14,12},{16,18},{18,... | collective-permute-start | bytes 3538952 | tf_op jit(solution)/shard_map/ppermute | solution.py:77
  474.9 50.9 %collective-permute-start.8 = (f32[2,2,2,2,24,768]{5,4,3,1,0,2:T(8,128)}, f32[2,2,2,2,24,768]{5,4,3,1,0,2:T(8,128)}, u32[]{:S(2)}, u32[]{:S(2)}) collective-permute-start(f32[2,2,2,2,24,768]{5,4,3,1,0,2:T(8,128)} %bitcast.374), channel_id=1, source_target_pairs={{0,2},{2,0},{4,6},{6,4},{8,10},{10,8},{12,14},{14,12},{16,18},{18,... | collective-permute-start | bytes 3538952 | tf_op jit(solution)/shard_map/ppermute | solution.py:77
  478.0 54.2 %collective-permute-start.1 = (f32[2,256,768]{2,1,0:T(8,128)}, f32[2,256,768]{2,1,0:T(8,128)}, u32[]{:S(2)}, u32[]{:S(2)}) collective-permute-start(f32[2,256,768]{2,1,0:T(8,128)} %convolution_add_fusion.2), channel_id=1, source_target_pairs={{1,0},{3,2},{5,4},{7,6},{9,8},{11,10},{13,12},{15,14},{17,16},{19,... | collective-permute-start | bytes 4718600 | tf_op jit(solution)/shard_map/ppermute | solution.py:26
  515.7 89.8 %collective-permute-start.32 = (f32[2,2,2,2,96,768]{5,4,3,2,1,0:T(8,128)}, f32[2,2,2,2,96,768]{5,4,3,2,1,0:T(8,128)}, u32[]{:S(2)}, u32[]{:S(2)}) collective-permute-start(f32[2,2,2,2,96,768]{5,4,3,2,1,0:T(8,128)} %dynamic-slice_bitcast_fusion), channel_id=1, source_target_pairs={{0,2},{2,0},{4,6},{6,4},{8,10},{10,8},{12,14},{14,12},{16,18},{18,... | collective-permute-start | bytes 14155784 | tf_op jit(solution)/shard_map/ppermute | solution.py:77
  517.8 18.7 %copy-start.41 = (bf16[96,8,2,512]{3,1,2,0:T(8,128)(2,1)}, bf16[96,8,2,512]{3,1,2,0:T(8,128)(2,1)S(1)}, u32[]{:S(2)}) copy-start(bf16[96,8,2,512]{3,1,2,0:T(8,128)(2,1)S(1)} %copy.187) | copy-start | bytes 4718596
  517.8 93.3 %collective-permute-start.26 = (f32[2,2,2,2,24,3072]{5,4,2,1,0,3:T(8,128)}, f32[2,2,2,2,24,3072]{5,4,2,1,0,3:T(8,128)}, u32[]{:S(2)}, u32[]{:S(2)}) collective-permute-start(f32[2,2,2,2,24,3072]{5,4,2,1,0,3:T(8,128)} %bitcast.371), channel_id=1, source_target_pairs={{0,2},{2,0},{4,6},{6,4},{8,10},{10,8},{12,14},{14,12},{16,18},{18,... | collective-permute-start | bytes 14155784 | tf_op jit(solution)/shard_map/ppermute | solution.py:77
  522.0 54.9 %collective-permute-start.21 = (f32[2,2,2,24,768]{4,3,1,0,2:T(8,128)}, f32[2,2,2,24,768]{4,3,1,0,2:T(8,128)}, u32[]{:S(2)}, u32[]{:S(2)}) collective-permute-start(f32[2,2,2,24,768]{4,3,1,0,2:T(8,128)} %bitcast.375), channel_id=1, source_target_pairs={{0,4},{2,6},{4,0},{6,2},{8,12},{10,14},{12,8},{14,10},{16,20},{18,... | collective-permute-start | bytes 1769480 | tf_op jit(solution)/shard_map/ppermute | solution.py:77
  525.8 52.4 %collective-permute-start.15 = (f32[2,2,2,24,768]{4,3,2,1,0:T(8,128)}, f32[2,2,2,24,768]{4,3,2,1,0:T(8,128)}, u32[]{:S(2)}, u32[]{:S(2)}) collective-permute-start(f32[2,2,2,24,768]{4,3,2,1,0:T(8,128)} %dynamic-slice_bitcast_fusion.8), channel_id=1, source_target_pairs={{0,1},{1,0},{2,3},{3,2},{4,5},{5,4},{6,7},{7,6},{8,9},{9,8},{10,11... | collective-permute-start | bytes 1769480 | tf_op jit(solution)/shard_map/ppermute | solution.py:77
  546.7 10.2 %copy-start.58 = (f32[1024]{0:T(1024)S(1)}, f32[1024]{0:T(1024)}, u32[]{:S(2)}) copy-start(f32[1024]{0:T(1024)} %copy-done.57) | copy-start | bytes 12292
  546.7 4.7 collective-permute-start.38
  551.5 3.7 collective-permute-start.39
  555.2 9.9 %collective-permute-start.40 = (f32[2,1,1,576]{3,1,2,0:T(1,128)S(1)}, f32[2,1,1,576]{3,1,2,0:T(1,128)S(1)}, u32[]{:S(2)}, u32[]{:S(2)}) collective-permute-start(f32[2,1,1,576]{3,1,2,0:T(1,128)S(1)} %fusion.116), channel_id=1, source_target_pairs={{0,8},{2,10},{4,12},{6,14},{8,0},{10,2},{12,4},{14,6},{16,24},{18,... | collective-permute-start | bytes 13832 | tf_op jit(solution)/shard_map/ppermute | solution.py:77
  565.2 5.8 collective-permute-start.41
  568.0 39.6 %slice-start.2 = ((s8[9437184]{0:T(1024)(128)(4,1)}), s8[4194304]{0:T(1024)(128)(4,1)S(1)}, s32[]{:S(2)}) async-start(s8[9437184]{0:T(1024)(128)(4,1)} %bitcast.404), calls=%async_computation.5 | async-start | bytes 8388608
  568.0 39.6 %slice-start.3 = ((s8[9437184]{0:T(1024)(128)(4,1)}), s8[4194304]{0:T(1024)(128)(4,1)S(1)}, s32[]{:S(2)}) async-start(s8[9437184]{0:T(1024)(128)(4,1)} %bitcast.404), calls=%async_computation.6 | async-start | bytes 8388608
  571.1 18.0 %copy-start.32 = (f32[2,2,2,2,24,768]{5,4,3,1,0,2:T(8,128)S(1)}, f32[2,2,2,2,24,768]{5,4,3,1,0,2:T(8,128)}, u32[]{:S(2)}) copy-start(f32[2,2,2,2,24,768]{5,4,3,1,0,2:T(8,128)} %copy-done.31) | copy-start | bytes 3538948
  571.1 3.7 collective-permute-start.42
  574.8 13.5 %collective-permute-start.9 = (f32[2,2,2,24,768]{4,3,2,1,0:T(8,128)S(1)}, f32[2,2,2,24,768]{4,3,2,1,0:T(8,128)S(1)}, u32[]{:S(2)}, u32[]{:S(2)}) collective-permute-start(f32[2,2,2,24,768]{4,3,2,1,0:T(8,128)S(1)} %copy-done.51), channel_id=1, source_target_pairs={{0,4},{2,6},{4,0},{6,2},{8,12},{10,14},{12,8},{14,10},{16,20},{18,... | collective-permute-start | bytes 1769480 | tf_op jit(solution)/shard_map/ppermute | solution.py:77
  576.8 38.9 %collective-permute-start.2 = (f32[2,2,2,2,24,768]{5,4,3,2,1,0:T(8,128)S(1)}, f32[2,2,2,2,24,768]{5,4,3,2,1,0:T(8,128)S(1)}, u32[]{:S(2)}, u32[]{:S(2)}) collective-permute-start(f32[2,2,2,2,24,768]{5,4,3,2,1,0:T(8,128)S(1)} %dynamic-slice_bitcast_fusion.5), channel_id=1, source_target_pairs={{0,2},{2,0},{4,6},{6,4},{8,10},{10,8},{12,14},{14,12},{16,18},{18,... | collective-permute-start | bytes 3538952 | tf_op jit(solution)/shard_map/ppermute | solution.py:77
  578.1 29.4 %slice-start.4 = ((s8[9437184]{0:T(1024)(128)(4,1)}), s8[1048576]{0:T(1024)(128)(4,1)S(1)}, s32[]{:S(2)}) async-start(s8[9437184]{0:T(1024)(128)(4,1)} %bitcast.404), calls=%async_computation.7 | async-start | bytes 2097152
  578.1 11.0 %collective-permute-start.22 = (f32[2,2,24,768]{3,2,1,0:T(8,128)S(1)}, f32[2,2,24,768]{3,2,1,0:T(8,128)S(1)}, u32[]{:S(2)}, u32[]{:S(2)}) collective-permute-start(f32[2,2,24,768]{3,2,1,0:T(8,128)S(1)} %dynamic-slice_bitcast_fusion.12), channel_id=1, source_target_pairs={{0,1},{1,0},{2,3},{3,2},{4,5},{5,4},{6,7},{7,6},{8,9},{9,8},{10,11... | collective-permute-start | bytes 884744 | tf_op jit(solution)/shard_map/ppermute | solution.py:77
  588.3 6.7 collective-permute-start.16
  589.2 7.0 collective-permute-start.10
  595.0 7.1 collective-permute-start.23
  596.2 8.3 %collective-permute-start.17 = (f32[2,24,768]{2,1,0:T(8,128)S(1)}, f32[2,24,768]{2,1,0:T(8,128)S(1)}, u32[]{:S(2)}, u32[]{:S(2)}) collective-permute-start(f32[2,24,768]{2,1,0:T(8,128)S(1)} %dynamic-slice_bitcast_fusion.17), channel_id=1, source_target_pairs={{0,8},{2,10},{4,12},{6,14},{8,0},{10,2},{12,4},{14,6},{16,24},{18,... | collective-permute-start | bytes 442376 | tf_op jit(solution)/shard_map/ppermute | solution.py:77
  602.1 13.0 %collective-permute-start.11 = (f32[2,24,768]{2,1,0:T(8,128)S(1)}, f32[2,24,768]{2,1,0:T(8,128)S(1)}, u32[]{:S(2)}, u32[]{:S(2)}) collective-permute-start(f32[2,24,768]{2,1,0:T(8,128)S(1)} %dynamic-slice_bitcast_fusion.18), channel_id=1, source_target_pairs={{0,8},{2,10},{4,12},{6,14},{8,0},{10,2},{12,4},{14,6},{16,24},{18,... | collective-permute-start | bytes 442376 | tf_op jit(solution)/shard_map/ppermute | solution.py:77
  604.5 13.1 %collective-permute-start.24 = (f32[24,768]{1,0:T(8,128)S(1)}, f32[24,768]{1,0:T(8,128)S(1)}, u32[]{:S(2)}, u32[]{:S(2)}) collective-permute-start(f32[24,768]{1,0:T(8,128)S(1)} %dynamic-slice_bitcast_fusion.20), channel_id=1, source_target_pairs={{0,16},{2,18},{4,20},{6,22},{8,24},{10,26},{12,28},{14,30},{16,0},... | collective-permute-start | bytes 221192 | tf_op jit(solution)/shard_map/ppermute | solution.py:77
  605.5 13.7 %collective-permute-start.18 = (f32[24,768]{1,0:T(8,128)S(1)}, f32[24,768]{1,0:T(8,128)S(1)}, u32[]{:S(2)}, u32[]{:S(2)}) collective-permute-start(f32[24,768]{1,0:T(8,128)S(1)} %dynamic-slice_bitcast_fusion.21), channel_id=1, source_target_pairs={{0,16},{2,18},{4,20},{6,22},{8,24},{10,26},{12,28},{14,30},{16,0},... | collective-permute-start | bytes 221192 | tf_op jit(solution)/shard_map/ppermute | solution.py:77
  611.2 72.0 %collective-permute-start.33 = (f32[2,2,2,96,768]{4,3,1,0,2:T(8,128)S(1)}, f32[2,2,2,96,768]{4,3,1,0,2:T(8,128)S(1)}, u32[]{:S(2)}, u32[]{:S(2)}) collective-permute-start(f32[2,2,2,96,768]{4,3,1,0,2:T(8,128)S(1)} %bitcast.418), channel_id=1, source_target_pairs={{0,4},{2,6},{4,0},{6,2},{8,12},{10,14},{12,8},{14,10},{16,20},{18,... | collective-permute-start | bytes 7077896 | tf_op jit(solution)/shard_map/ppermute | solution.py:77
  615.2 70.5 %collective-permute-start.27 = (f32[2,2,2,24,3072]{4,3,2,1,0:T(8,128)S(1)}, f32[2,2,2,24,3072]{4,3,2,1,0:T(8,128)S(1)}, u32[]{:S(2)}, u32[]{:S(2)}) collective-permute-start(f32[2,2,2,24,3072]{4,3,2,1,0:T(8,128)S(1)} %dynamic-slice_bitcast_fusion.1), channel_id=1, source_target_pairs={{0,1},{1,0},{2,3},{3,2},{4,5},{5,4},{6,7},{7,6},{8,9},{9,8},{10,11... | collective-permute-start | bytes 7077896 | tf_op jit(solution)/shard_map/ppermute | solution.py:77
  615.7 6.1 collective-permute-start.12
  617.7 65.2 %collective-permute-start.3 = (f32[2,2,2,24,768]{4,3,1,0,2:T(8,128)S(1)}, f32[2,2,2,24,768]{4,3,1,0,2:T(8,128)S(1)}, u32[]{:S(2)}, u32[]{:S(2)}) collective-permute-start(f32[2,2,2,24,768]{4,3,1,0,2:T(8,128)S(1)} %bitcast.431), channel_id=1, source_target_pairs={{0,1},{1,0},{2,3},{3,2},{4,5},{5,4},{6,7},{7,6},{8,9},{9,8},{10,11... | collective-permute-start | bytes 1769480 | tf_op jit(solution)/shard_map/ppermute | solution.py:77
  619.2 63.0 %collective-permute-start.25 = (f32[24,768]{1,0:T(8,128)S(1)}, f32[24,768]{1,0:T(8,128)S(1)}, u32[]{:S(2)}, u32[]{:S(2)}) collective-permute-start(f32[24,768]{1,0:T(8,128)S(1)} %bitcast_add_fusion.29), channel_id=1, source_target_pairs={{0,1},{1,0},{2,3},{3,2},{4,5},{5,4},{6,7},{7,6},{8,9},{9,8},{10,11... | collective-permute-start | bytes 221192 | tf_op jit(solution)/shard_map/ppermute | solution.py:77
  621.8 69.4 %collective-permute-start.19 = (f32[24,768]{1,0:T(8,128)S(1)}, f32[24,768]{1,0:T(8,128)S(1)}, u32[]{:S(2)}, u32[]{:S(2)}) collective-permute-start(f32[24,768]{1,0:T(8,128)S(1)} %bitcast_add_fusion.30), channel_id=1, source_target_pairs={{0,1},{1,0},{2,3},{3,2},{4,5},{5,4},{6,7},{7,6},{8,9},{9,8},{10,11... | collective-permute-start | bytes 221192 | tf_op jit(solution)/shard_map/ppermute | solution.py:77
  682.2 9.1 %collective-permute-start.13 = (f32[24,768]{1,0:T(8,128)S(1)}, f32[24,768]{1,0:T(8,128)S(1)}, u32[]{:S(2)}, u32[]{:S(2)}) collective-permute-start(f32[24,768]{1,0:T(8,128)S(1)} %bitcast_add_fusion.31), channel_id=1, source_target_pairs={{0,1},{1,0},{2,3},{3,2},{4,5},{5,4},{6,7},{7,6},{8,9},{9,8},{10,11... | collective-permute-start | bytes 221192 | tf_op jit(solution)/shard_map/ppermute | solution.py:77
  683.0 6.8 collective-permute-start.4
  683.6 20.8 %collective-permute-start.34 = (f32[2,2,96,768]{3,2,1,0:T(8,128)S(1)}, f32[2,2,96,768]{3,2,1,0:T(8,128)S(1)}, u32[]{:S(2)}, u32[]{:S(2)}) collective-permute-start(f32[2,2,96,768]{3,2,1,0:T(8,128)S(1)} %dynamic-slice_bitcast_fusion.2), channel_id=1, source_target_pairs={{0,1},{1,0},{2,3},{3,2},{4,5},{5,4},{6,7},{7,6},{8,9},{9,8},{10,11... | collective-permute-start | bytes 3538952 | tf_op jit(solution)/shard_map/ppermute | solution.py:77
  686.1 19.4 %collective-permute-start.28 = (f32[2,2,24,3072]{3,2,1,0:T(8,128)S(1)}, f32[2,2,24,3072]{3,2,1,0:T(8,128)S(1)}, u32[]{:S(2)}, u32[]{:S(2)}) collective-permute-start(f32[2,2,24,3072]{3,2,1,0:T(8,128)S(1)} %dynamic-slice_bitcast_fusion.3), channel_id=1, source_target_pairs={{0,4},{2,6},{4,0},{6,2},{8,12},{10,14},{12,8},{14,10},{16,20},{18,... | collective-permute-start | bytes 3538952 | tf_op jit(solution)/shard_map/ppermute | solution.py:77
  689.8 5.2 collective-permute-start.5
  695.1 11.9 %collective-permute-start.6 = (f32[24,768]{1,0:T(8,128)S(1)}, f32[24,768]{1,0:T(8,128)S(1)}, u32[]{:S(2)}, u32[]{:S(2)}) collective-permute-start(f32[24,768]{1,0:T(8,128)S(1)} %dynamic-slice_bitcast_fusion.23), channel_id=1, source_target_pairs={{0,16},{2,18},{4,20},{6,22},{8,24},{10,26},{12,28},{14,30},{16,0},... | collective-permute-start | bytes 221192 | tf_op jit(solution)/shard_map/ppermute | solution.py:77
  704.6 15.8 %collective-permute-start.35 = (f32[2,96,768]{2,1,0:T(8,128)S(1)}, f32[2,96,768]{2,1,0:T(8,128)S(1)}, u32[]{:S(2)}, u32[]{:S(2)}) collective-permute-start(f32[2,96,768]{2,1,0:T(8,128)S(1)} %dynamic-slice_bitcast_fusion.6), channel_id=1, source_target_pairs={{0,8},{2,10},{4,12},{6,14},{8,0},{10,2},{12,4},{14,6},{16,24},{18,... | collective-permute-start | bytes 1769480 | tf_op jit(solution)/shard_map/ppermute | solution.py:77
  705.7 27.3 %collective-permute-start.29 = (f32[2,24,3072]{2,1,0:T(8,128)S(1)}, f32[2,24,3072]{2,1,0:T(8,128)S(1)}, u32[]{:S(2)}, u32[]{:S(2)}) collective-permute-start(f32[2,24,3072]{2,1,0:T(8,128)S(1)} %dynamic-slice_bitcast_fusion.7), channel_id=1, source_target_pairs={{0,8},{2,10},{4,12},{6,14},{8,0},{10,2},{12,4},{14,6},{16,24},{18,... | collective-permute-start | bytes 1769480 | tf_op jit(solution)/shard_map/ppermute | solution.py:77
  707.0 26.3 %collective-permute-start.7 = (f32[24,768]{1,0:T(8,128)S(1)}, f32[24,768]{1,0:T(8,128)S(1)}, u32[]{:S(2)}, u32[]{:S(2)}) collective-permute-start(f32[24,768]{1,0:T(8,128)S(1)} %bitcast_add_fusion.32), channel_id=1, source_target_pairs={{0,1},{1,0},{2,3},{3,2},{4,5},{5,4},{6,7},{7,6},{8,9},{9,8},{10,11... | collective-permute-start | bytes 221192 | tf_op jit(solution)/shard_map/ppermute | solution.py:77
  720.5 12.7 %collective-permute-start.36 = (f32[96,768]{1,0:T(8,128)S(1)}, f32[96,768]{1,0:T(8,128)S(1)}, u32[]{:S(2)}, u32[]{:S(2)}) collective-permute-start(f32[96,768]{1,0:T(8,128)S(1)} %dynamic-slice_bitcast_fusion.10), channel_id=1, source_target_pairs={{0,16},{2,18},{4,20},{6,22},{8,24},{10,26},{12,28},{14,30},{16,0},... | collective-permute-start | bytes 884744 | tf_op jit(solution)/shard_map/ppermute | solution.py:77
  733.1 17.7 %copy-start.1 = (bf16[768,768]{1,0:T(8,128)(2,1)S(1)}, bf16[768,768]{1,0:T(8,128)(2,1)}, u32[]{:S(2)}) copy-start(bf16[768,768]{1,0:T(8,128)(2,1)} %param.23) | copy-start | bytes 3538948
  733.2 9.9 %collective-permute-start.30 = (f32[24,3072]{1,0:T(8,128)S(1)}, f32[24,3072]{1,0:T(8,128)S(1)}, u32[]{:S(2)}, u32[]{:S(2)}) collective-permute-start(f32[24,3072]{1,0:T(8,128)S(1)} %dynamic-slice_bitcast_fusion.11), channel_id=1, source_target_pairs={{0,16},{2,18},{4,20},{6,22},{8,24},{10,26},{12,28},{14,30},{16,0},... | collective-permute-start | bytes 884744 | tf_op jit(solution)/shard_map/ppermute | solution.py:77
  733.3 10.6 %collective-permute-start.37 = (f32[96,768]{1,0:T(8,128)S(1)}, f32[96,768]{1,0:T(8,128)S(1)}, u32[]{:S(2)}, u32[]{:S(2)}) collective-permute-start(f32[96,768]{1,0:T(8,128)S(1)} %bitcast_add_fusion.19), channel_id=1, source_target_pairs={{0,1},{1,0},{2,3},{3,2},{4,5},{5,4},{6,7},{7,6},{8,9},{9,8},{10,11... | collective-permute-start | bytes 884744 | tf_op jit(solution)/shard_map/ppermute | solution.py:77
  743.1 6.8 collective-permute-start.31
  (76 other events, 355.6 us)
Sparse Core Ops, SparseCore 0:
  9.6 29.8 all-gather.1
  551.5 25.6 reduce-scatter.1
